TPU v7x, 128 devices: a whole 4x4x4 slice. The times are simulated.
128 devices in a mesh: tok: 4 (over x), exp: 32 (over y, z, core).
Axes of the slice: x: 4, y: 4, z: 4, core: 2. Of those that a mesh axis runs over, the one named last changes fastest.
Arguments:
- captured: bfloat16 [8192, 8, 1024], P(('tok', 'exp')), may hold values from -16 to 16
- expert_ids: int32 [8192, 8], P(('tok', 'exp')), may hold values from 0 to 127, all different within a row; in each aligned block of 32 rows (0 to 31, 32 to 63, ...) at most 4 rows name the same one
Outputs:
- whitening: float32 [128, 1024, 1024], P(('tok', 'exp'))
Inputs may be any that keep to these rules, and one draw needn't show every extreme that they name: `expert_ids`: each row names 8 different experts; every expert is named by some row. In each aligned block of 32 token rows no expert is named more than 4 times, and in some block some expert is named exactly 4 times.
All inputs are finite; a program needn't handle non-finite values.
Results may differ from a plain program's by a relative error of at most 0.0003.
Values may be sent and summed in bfloat16 or wider, within the bound.
No kernel may reach another device: no remote copies, remote signals or barrier semaphores. Data moves between devices by JAX's collectives and lax.ppermute only.
A program may use at most 64 MiB of HBM per device.

v0:
```python
import jax
import jax.numpy as jnp
from jax import lax
from jax.sharding import PartitionSpec as P

damping = 0.1


def whiten(gram, count):
    hess = gram / count
    shift = damping * jnp.mean(jnp.diagonal(hess))
    identity = jnp.eye(hess.shape[0], dtype=hess.dtype)
    hess = hess + shift * identity
    factor = jnp.linalg.cholesky(hess)
    return lax.linalg.triangular_solve(factor, identity, left_side=True, lower=True)


def gram_total(arrived):
    feature_width = arrived.shape[2]
    stacked = arrived.reshape(-1, feature_width)
    return lax.dot_general(
        stacked, stacked, (((0,), (0,)), ((), ())), preferred_element_type=jnp.float32
    )


def count_rows(arrived_counts):
    return jnp.sum(arrived_counts.astype(jnp.float32))


def shards(captured, expert_ids):
    tok_size = lax.axis_size("tok")
    exp_size = lax.axis_size("exp")
    device_count = tok_size * exp_size
    token_rows, top_count, feature_width = captured.shape
    half_rows = token_rows // 2
    block_entries = half_rows * top_count
    slot_cap = 2 * block_entries // device_count
    flat_rows = captured.reshape(token_rows * top_count, feature_width)
    flat_ids = expert_ids.reshape(-1)
    expert_iota = lax.broadcasted_iota(jnp.int32, (1, device_count), 1)
    earlier = (
        lax.broadcasted_iota(jnp.int32, (block_entries, block_entries), 1)
        < lax.broadcasted_iota(jnp.int32, (block_entries, block_entries), 0)
    ).astype(jnp.float32)
    positions = []
    half_counts = []
    for part_index in range(2):
        block_ids = flat_ids[part_index * block_entries : (part_index + 1) * block_entries]
        onehot = (block_ids[:, None] == expert_iota).astype(jnp.float32)
        before = jnp.dot(earlier, onehot, precision=lax.Precision.HIGHEST)
        rank_in_block = jnp.sum(before * onehot, axis=1).astype(jnp.int32)
        positions.append(block_ids * (2 * slot_cap) + part_index * slot_cap + rank_in_block)
        half_counts.append(jnp.sum(onehot, axis=0))
    send_counts = jnp.stack(half_counts, axis=1).astype(jnp.bfloat16)
    slot_target = jnp.concatenate(positions)
    outbox = (
        jnp.zeros((device_count * 2 * slot_cap, feature_width), jnp.bfloat16)
        .at[slot_target]
        .set(flat_rows)
    )
    outbox = outbox.reshape(device_count, 2 * slot_cap, feature_width)
    arrived, arrived_counts = (
        lax.all_to_all(outbox, ("tok", "exp"), split_axis=0, concat_axis=0, tiled=True),
        lax.all_to_all(send_counts, ("tok", "exp"), split_axis=0, concat_axis=0, tiled=True),
    )
    gram_sum = gram_total(arrived)
    live_rows = count_rows(arrived_counts)
    return whiten(gram_sum, live_rows)[None]


def solution(mesh):
    placed = (P(("tok", "exp"), None, None), P(("tok", "exp"), None))
    return jax.shard_map(
        shards, mesh=mesh, in_specs=placed, out_specs=P(("tok", "exp"), None, None), check_vma=False
    )
```

profile of v0, /device:TPU:1, one launch (start us, length us, event | category | flops | bytes accessed | tf_op | source)
XLA Modules:
  0.0 434.2 jit_solution(11295845801572058209)
XLA Ops:
  2.2 11.5 %all-to-all-start.1 = ((bf16[128,1,2]{2,1,0:T(2,128)(2,1)}), bf16[128,1,2]{2,1,0:T(2,128)(2,1)S(1)}, u32[]{:S(2)}, u32[]{:S(2)}) async-start(bf16[128,1,2]{2,1,0:T(2,128)(2,1)} %copy.14), calls=%async_computation.1 | async-start | bytes 131072 | tf_op jit(solution)/shard_map/all_to_all | solution.py:64
  23.1 5.1 %all-to-all-start = ((bf16[128,8,1024]{2,1,0:T(8,128)(2,1)}), bf16[128,8,1024]{2,1,0:T(8,128)(2,1)S(1)}, u32[]{:S(2)}, u32[]{:S(2)}) async-start(bf16[128,8,1024]{2,1,0:T(8,128)(2,1)} %bitcast.4), calls=%async_computation | async-start | bytes 4194304 | tf_op jit(solution)/shard_map/all_to_all | solution.py:63
  32.7 25.9 %all-to-all-done = bf16[128,8,1024]{2,1,0:T(8,128)(2,1)S(1)} async-done(((bf16[128,8,1024]{2,1,0:T(8,128)(2,1)}), bf16[128,8,1024]{2,1,0:T(8,128)(2,1)S(1)}, u32[]{:S(2)}, u32[]{:S(2)}) %all-to-all-start) | async-done | bytes 2097184 | tf_op jit(solution)/shard_map/all_to_all | solution.py:63
  58.7 5.1 %bitcast_divide_fusion = f32[1024,1024]{1,0:T(8,128)} fusion(bf16[128,8,1024]{2,1,0:T(8,128)(2,1)S(1)} %all-to-all-done, f32[]{:T(128)} %convert_reduce_fusion.2), kind=kOutput, calls=%fused_computation.5 | convolution fusion | flops 2148532224 | bytes 6291460 | tf_op jit(solution)/shard_map/dot_general | solution.py:21
  63.7 16.8 %gather_fusion = f32[1024]{0:T(1024)S(1)} fusion(f32[1024,1024]{1,0:T(8,128)} %bitcast_divide_fusion, s32[1024]{0:T(1024)S(1)} %bitcast.118), kind=kCustom, calls=%fused_computation | custom fusion | bytes 16384 | tf_op jit(solution)/shard_map/jit(diagonal)/cond/branch_0_fun/gather | solution.py:11
  80.5 5.8 %copy.15 = f32[1024,1024]{1,0:T(8,128)} copy(f32[1024,1024]{0,1:T(8,128)} %bitcast.119) | data formatting | bytes 8388608 | tf_op jit(solution)/shard_map/div | solution.py:10
  93.9 11.7 %cholesky.222 = f32[128,128]{1,0:T(8,128)S(1)} custom-call(f32[128,128]{1,0:T(8,128)S(1)} %cholesky.577), custom_call_target="Cholesky" | custom-call | tf_op jit(solution)/shard_map/jit(cholesky)/cholesky | solution.py:14
  108.2 9.8 %custom-call.62 = f32[1,128,128]{1,2,0:T(8,128)S(1)} custom-call(f32[1,128,128]{2,1,0:T(8,128)S(1)} %get-tuple-element.69), custom_call_target="InvertDiagBlocksLowerTriangular" | custom-call | tf_op jit(solution)/shard_map/jit(cholesky)/cholesky | solution.py:14
  121.9 11.9 %cholesky.243 = f32[128,128]{1,0:T(8,128)S(1)} custom-call(f32[128,128]{1,0:T(8,128)S(1)} %cholesky.581), custom_call_target="Cholesky" | custom-call | tf_op jit(solution)/shard_map/jit(cholesky)/cholesky | solution.py:14
  134.4 9.8 %custom-call.63 = f32[1,128,128]{1,2,0:T(8,128)S(1)} custom-call(f32[1,128,128]{2,1,0:T(8,128)S(1)} %get-tuple-element.66), custom_call_target="InvertDiagBlocksLowerTriangular" | custom-call | tf_op jit(solution)/shard_map/jit(cholesky)/cholesky | solution.py:14
  147.5 11.7 %cholesky.466 = f32[128,128]{1,0:T(8,128)S(1)} custom-call(f32[128,128]{1,0:T(8,128)S(1)} %cholesky.586), custom_call_target="Cholesky" | custom-call | tf_op jit(solution)/shard_map/jit(cholesky)/cholesky | solution.py:14
  160.5 9.8 %custom-call.64 = f32[1,128,128]{1,2,0:T(8,128)S(1)} custom-call(f32[1,128,128]{2,1,0:T(8,128)S(1)} %get-tuple-element.63), custom_call_target="InvertDiagBlocksLowerTriangular" | custom-call | tf_op jit(solution)/shard_map/jit(cholesky)/cholesky | solution.py:14
  173.8 11.9 %cholesky.485 = f32[128,128]{1,0:T(8,128)S(1)} custom-call(f32[128,128]{1,0:T(8,128)S(1)} %cholesky.591), custom_call_target="Cholesky" | custom-call | tf_op jit(solution)/shard_map/jit(cholesky)/cholesky | solution.py:14
  187.1 9.8 %custom-call.65 = f32[1,128,128]{1,2,0:T(8,128)S(1)} custom-call(f32[1,128,128]{2,1,0:T(8,128)S(1)} %get-tuple-element.60), custom_call_target="InvertDiagBlocksLowerTriangular" | custom-call | tf_op jit(solution)/shard_map/jit(cholesky)/cholesky | solution.py:14
  200.3 11.7 %cholesky.504 = f32[128,128]{1,0:T(8,128)S(1)} custom-call(f32[128,128]{1,0:T(8,128)S(1)} %cholesky.596), custom_call_target="Cholesky" | custom-call | tf_op jit(solution)/shard_map/jit(cholesky)/cholesky | solution.py:14
  213.3 10.2 %custom-call.66 = f32[1,128,128]{1,2,0:T(8,128)S(1)} custom-call(f32[1,128,128]{2,1,0:T(8,128)S(1)} %get-tuple-element.57), custom_call_target="InvertDiagBlocksLowerTriangular" | custom-call | tf_op jit(solution)/shard_map/jit(cholesky)/cholesky | solution.py:14
  226.8 11.7 %cholesky.524 = f32[128,128]{1,0:T(8,128)S(1)} custom-call(f32[128,128]{1,0:T(8,128)S(1)} %cholesky.601), custom_call_target="Cholesky" | custom-call | tf_op jit(solution)/shard_map/jit(cholesky)/cholesky | solution.py:14
  239.9 9.8 %custom-call.67 = f32[1,128,128]{1,2,0:T(8,128)S(1)} custom-call(f32[1,128,128]{2,1,0:T(8,128)S(1)} %get-tuple-element.54), custom_call_target="InvertDiagBlocksLowerTriangular" | custom-call | tf_op jit(solution)/shard_map/jit(cholesky)/cholesky | solution.py:14
  252.7 11.9 %cholesky.544 = f32[128,128]{1,0:T(8,128)S(1)} custom-call(f32[128,128]{1,0:T(8,128)S(1)} %cholesky.606), custom_call_target="Cholesky" | custom-call | tf_op jit(solution)/shard_map/jit(cholesky)/cholesky | solution.py:14
  265.9 9.8 %custom-call.68 = f32[1,128,128]{1,2,0:T(8,128)S(1)} custom-call(f32[1,128,128]{2,1,0:T(8,128)S(1)} %get-tuple-element.51), custom_call_target="InvertDiagBlocksLowerTriangular" | custom-call | tf_op jit(solution)/shard_map/jit(cholesky)/cholesky | solution.py:14
  278.3 11.7 %cholesky.562 = f32[128,128]{1,0:T(8,128)S(1)} custom-call(f32[128,128]{1,0:T(8,128)S(1)} %convolution_subtract_fusion.11), custom_call_target="Cholesky" | custom-call | tf_op jit(solution)/shard_map/jit(cholesky)/cholesky | solution.py:14
  297.1 4.9 %select_select_fusion = f32[1024,1024]{1,0:T(8,128)} fusion(f32[1024,1024]{1,0:T(8,128)} %get-tuple-element.49, pred[]{:T(512)S(6)} %cholesky.576), kind=kLoop, calls=%fused_computation.4 | loop fusion | flops 4194304 | bytes 8388609 | tf_op jit(solution)/shard_map/triangular_solve | solution.py:15
  302.0 27.6 %while.1 = (s32[]{:T(128)}, f32[1024,1024]{1,0:T(8,128)}, s32[8,2]{0,1:T(2,128)S(1)}, f32[8,128,128]{2,1,0:T(8,128)}, s32[]{:T(128)}) while((s32[]{:T(128)}, f32[1024,1024]{1,0:T(8,128)}, s32[8,2]{0,1:T(2,128)S(1)}, f32[8,128,128]{2,1,0:T(8,128)}, s32[]{:T(128)}) %tuple.58), condition=%wide.while_cond, body=%wide.while_body.sunk | while | flops 2 | bytes 132205 | solution.py:15
  329.6 79.6 %custom-call.69 = f32[8,128,128]{1,2,0:T(8,128)S(1)} custom-call(f32[8,128,128]{2,1,0:T(8,128)} %get-tuple-element.12), custom_call_target="InvertDiagBlocksLowerTriangular" | custom-call | tf_op jit(solution)/shard_map/triangular_solve | solution.py:15
  (109 shorter events, 110.1 us)
Async XLA Ops:
  0.0 14.2 %copy-start = (bf16[64,8,1024]{2,1,0:T(8,128)(2,1)S(1)}, bf16[64,8,1024]{2,1,0:T(8,128)(2,1)}, u32[]{:S(2)}) copy-start(bf16[64,8,1024]{2,1,0:T(8,128)(2,1)} %param.2) | copy-start | bytes 3145732
  2.2 20.9 %all-to-all-start.1 = ((bf16[128,1,2]{2,1,0:T(2,128)(2,1)}), bf16[128,1,2]{2,1,0:T(2,128)(2,1)S(1)}, u32[]{:S(2)}, u32[]{:S(2)}) async-start(bf16[128,1,2]{2,1,0:T(2,128)(2,1)} %copy.14), calls=%async_computation.1 | async-start | bytes 131072 | tf_op jit(solution)/shard_map/all_to_all | solution.py:64
  23.1 35.6 %all-to-all-start = ((bf16[128,8,1024]{2,1,0:T(8,128)(2,1)}), bf16[128,8,1024]{2,1,0:T(8,128)(2,1)S(1)}, u32[]{:S(2)}, u32[]{:S(2)}) async-start(bf16[128,8,1024]{2,1,0:T(8,128)(2,1)} %bitcast.4), calls=%async_computation | async-start | bytes 4194304 | tf_op jit(solution)/shard_map/all_to_all | solution.py:63
  91.9 2.0 copy-start.2
  409.2 3.9 copy-start.1
  432.0 2.0 copy-start.3
where the time goes:
time: 442 us; the launch traced here: 434 us
  other arithmetic  267 us (60%)
  local copies, waits for them, and re-layouts  62.9 us (14%)
  matrix products  51.1 us (12%)
  waiting for transfers between devices  30.6 us (7%)
  starting transfers between devices  16.6 us (4%)
  between operations  6.29 us (1%)
    another operation x30, other arithmetic, whiten(): factor = jnp.linalg.cholesky(hess)  172 us
    another operation x3, other arithmetic, whiten(): lax.linalg.triangular_solve(factor, identity, left_side=True, lower=True)  84.5 us
    another operation x24, local copies, waits for them, and re-layouts  27.6 us
    all_to_all x1, waiting for transfers between devices, shards(): lax.all_to_all(outbox, ('tok', 'exp'), split_axis=0, concat_axis=0, tiled...  25.9 us
    another operation x14, matrix products, whiten(): factor = jnp.linalg.cholesky(hess)  22.9 us
    another operation x15, matrix products, whiten(): lax.linalg.triangular_solve(factor, identity, left_side=True, lower=True)  22.6 us
    gather x1, local copies, waits for them, and re-layouts, whiten(): shift = damping * jnp.mean(jnp.diagonal(hess))  16.8 us
    all_to_all x1, starting transfers between devices, shards(): lax.all_to_all(send_counts, ('tok', 'exp'), split_axis=0, concat_axis=0,...  11.5 us
  transfers between devices with their start and end apart: 2, of which 2 were waited for; matrix products, arithmetic and copies ran while one was open for 2% of the time, Pallas kernels for 0%

commit v1 on v0

v1 whole, which is shorter than its diff:
```python
import jax
import jax.numpy as jnp
from jax import lax
from jax.experimental import pallas as pl
from jax.experimental.pallas import tpu as pltpu
from jax.sharding import PartitionSpec as P

damping = 0.1
EMPTY = 32.0
BLOCK = 128
PANEL = 8
F32 = jnp.float32
BF16 = jnp.bfloat16


def iota(shape, dim):
    return lax.broadcasted_iota(jnp.int32, shape, dim)


def route_kernel(slots_per_pair, ids_ref, rows_ref, out_ref, slot_ref):
    tokens, top = ids_ref.shape
    entries = tokens * top
    half = entries // 2
    tile = out_ref.shape[0]

    @pl.when(pl.program_id(0) == 0)
    def _():
        ids = ids_ref[...].astype(F32).astype(BF16)
        pick_col = (iota((entries, tokens), 0) // top == iota((entries, tokens), 1)).astype(F32).astype(BF16)
        by_col = jnp.dot(pick_col, ids, preferred_element_type=F32)
        keep = iota((entries, top), 0) % top == iota((entries, top), 1)
        id_col = jnp.sum(jnp.where(keep, by_col, 0.0), axis=1, keepdims=True)
        pick_row = (iota((tokens, entries), 1) // top == iota((tokens, entries), 0)).astype(F32).astype(BF16)
        by_row = lax.dot_general(ids, pick_row, (((0,), (0,)), ((), ())), preferred_element_type=F32)
        keep = iota((top, entries), 1) % top == iota((top, entries), 0)
        id_row = jnp.sum(jnp.where(keep, by_row, 0.0), axis=0, keepdims=True)
        earlier = iota((half, half), 0) < iota((half, half), 1)
        for part in range(2):
            col = id_col[part * half : (part + 1) * half]
            row = id_row[:, part * half : (part + 1) * half]
            rank = jnp.sum(jnp.where((col == row) & earlier, 1.0, 0.0), axis=0, keepdims=True)
            slot = row * slots_per_pair + rank + part * (slots_per_pair // 2)
            slot_ref[:, part * half : (part + 1) * half] = slot.astype(jnp.int32)

    first = pl.program_id(0) * tile
    onehot = jnp.where(iota((tile, entries), 0) + first == slot_ref[...], 1.0, 0.0)
    used = jnp.sum(onehot, axis=1, keepdims=True)
    moved = jnp.dot(onehot.astype(BF16), rows_ref[...], preferred_element_type=F32)
    mark = jnp.where(iota((tile, BLOCK), 1) == 0, EMPTY * (1.0 - used), 0.0)
    out_ref[:, :BLOCK] = (moved[:, :BLOCK] + mark).astype(BF16)
    out_ref[:, BLOCK:] = moved[:, BLOCK:].astype(BF16)


def route(captured, expert_ids, device_count):
    token_rows, top, width = captured.shape
    per_pair = token_rows * top * 2 // device_count
    slots = per_pair * device_count
    tile = 256
    return pl.pallas_call(
        lambda *refs: route_kernel(per_pair, *refs),
        grid=(slots // tile,),
        out_shape=jax.ShapeDtypeStruct((slots, width), BF16),
        in_specs=[
            pl.BlockSpec((token_rows, top), lambda i: (0, 0)),
            pl.BlockSpec((token_rows * top, width), lambda i: (0, 0)),
        ],
        out_specs=pl.BlockSpec((tile, width), lambda i: (i, 0)),
        scratch_shapes=[pltpu.VMEM((1, token_rows * top), jnp.int32)],
        compiler_params=pltpu.CompilerParams(vmem_limit_bytes=32 * 2**20),
        name="route",
    )(expert_ids, captured.reshape(token_rows * top, width))


LEFT = (0, 0, 1, 1, 0, 2)
RIGHT = (0, 1, 0, 1, 2, 0)


def pieces(x):
    first = x.astype(BF16)
    rest = x - first.astype(F32)
    second = rest.astype(BF16)
    third = (rest - second.astype(F32)).astype(BF16)
    return first, second, third


def left_stack(x):
    part = pieces(x)
    return jnp.concatenate([part[i] for i in LEFT], axis=1)


def right_stack(x, axis):
    part = pieces(x)
    return jnp.concatenate([part[i] for i in RIGHT], axis=axis)


def along_lanes(x, lane):
    return jnp.broadcast_to(x[:, lane : lane + 1], x.shape)


def along_sublanes(x, row):
    return jnp.broadcast_to(x[row : row + 1, :], x.shape)


def invert_factor(rows):
    lane = iota((PANEL, BLOCK), 1)
    sub = iota((PANEL, BLOCK), 0)
    rows = list(rows)
    count = len(rows)
    for p in range(count):
        base = p * PANEL
        corner = [along_lanes(rows[p], base + j) for j in range(PANEL)]
        below = {i: [along_lanes(rows[i], base + j) for j in range(PANEL)] for i in range(p + 1, count)}
        inside = (lane >= base) & (lane < base + PANEL)
        forward = jnp.where(inside, jnp.where(lane == sub + base, 1.0, 0.0), rows[p])
        full = forward
        pivots = jnp.ones_like(forward)
        inverses = jnp.ones_like(forward)
        for j in range(PANEL):
            pivot = along_sublanes(corner[j], j)
            inverse = 1.0 / pivot
            multiplier = jnp.where(sub == j, 0.0, corner[j] * inverse)
            for c in range(j + 1, PANEL):
                corner[c] = corner[c] - multiplier * along_sublanes(corner[c], j)
            row = along_sublanes(forward, j)
            forward = forward - jnp.where(sub > j, multiplier, 0.0) * row
            full = full - multiplier * row
            pivots = jnp.where(sub == j, pivot, pivots)
            inverses = jnp.where(sub == j, inverse, inverses)
        root = lax.rsqrt(pivots)
        root = root * (1.5 - 0.5 * pivots * root * root)
        rows[p] = forward * root
        full = full * inverses
        steps = [along_sublanes(full, j) for j in range(PANEL)]
        for i in range(p + 1, count):
            terms = [below[i][j] * steps[j] for j in range(PANEL)]
            while len(terms) > 1:
                terms = [a + b for a, b in zip(terms[::2], terms[1::2])]
            rows[i] = jnp.where(inside, 0.0, rows[i]) - terms[0]
    return rows


def whiten_kernel(x_ref, t_ref, right_ref):
    width = t_ref.shape[0]
    blocks = width // BLOCK
    contract_rows = (((0,), (0,)), ((), ()))
    contract_lanes = (((1,), (1,)), ((), ()))

    def gram_tile(i, _):
        at = pl.ds(pl.multiple_of(i * 2 * BLOCK, 2 * BLOCK), 2 * BLOCK)
        t_ref[at, :] = lax.dot_general(x_ref[:, at], x_ref[...], contract_rows, preferred_element_type=F32)
        return 0

    lax.fori_loop(0, blocks // 2, gram_tile, 0)

    lane = iota((x_ref.shape[0], BLOCK), 1)
    head = x_ref[:, :BLOCK].astype(F32)
    filled = (lane == 0) & (head != EMPTY)
    rows_here = jnp.sum(jnp.where(filled, 1.0, 0.0))
    square = jnp.sum(jnp.where(filled, head * head, 0.0))
    corner = t_ref[:PANEL, :BLOCK]
    at_origin = (iota((PANEL, BLOCK), 0) == 0) & (iota((PANEL, BLOCK), 1) == 0)
    t_ref[:PANEL, :BLOCK] = jnp.where(at_origin, square, corner)

    eye = iota((BLOCK, BLOCK), 0) == iota((BLOCK, BLOCK), 1)

    def block(i):
        return pl.ds(pl.multiple_of(i * BLOCK, BLOCK), BLOCK)

    diagonal = jnp.zeros((BLOCK, BLOCK), F32)
    for k in range(blocks):
        diagonal = diagonal + jnp.where(eye, t_ref[block(k), block(k)], 0.0)
    shift = damping * (jnp.sum(diagonal) / width)
    scale = jnp.sqrt(rows_here)
    lower = iota((BLOCK, BLOCK), 0) >= iota((BLOCK, BLOCK), 1)
    columns = iota((BLOCK, width), 1)

    def step(k, _):
        mine = block(k)
        spd = t_ref[mine, mine] + jnp.where(eye, shift, 0.0)
        done = invert_factor([spd[p * PANEL : (p + 1) * PANEL] for p in range(BLOCK // PANEL)])
        inverse = jnp.where(lower, jnp.concatenate(done, axis=0), 0.0)
        inverse_right = right_stack(inverse, 1)
        t_ref[mine, mine] = jnp.where(eye, 1.0, 0.0)
        solved = jnp.dot(left_stack(inverse), right_stack(t_ref[mine, :], 0), preferred_element_type=F32)
        right_ref[...] = right_stack(solved, 0)
        t_ref[mine, :] = jnp.where(columns < (k + 1) * BLOCK, solved * scale, 0.0)

        def update(i, _):
            panel = lax.dot_general(
                left_stack(t_ref[block(i), mine]), inverse_right, contract_lanes, preferred_element_type=F32
            )
            t_ref[block(i), mine] = jnp.zeros((BLOCK, BLOCK), F32)
            t_ref[block(i), :] -= jnp.dot(left_stack(panel), right_ref[...], preferred_element_type=F32)
            return 0

        lax.fori_loop(k + 1, blocks, update, 0)
        return 0

    lax.fori_loop(0, blocks, step, 0)


def whiten(arrived):
    width = arrived.shape[1]
    return pl.pallas_call(
        whiten_kernel,
        out_shape=jax.ShapeDtypeStruct((width, width), F32),
        in_specs=[pl.BlockSpec(memory_space=pltpu.VMEM)],
        out_specs=pl.BlockSpec(memory_space=pltpu.VMEM),
        scratch_shapes=[pltpu.VMEM((len(RIGHT) * BLOCK, width), BF16)],
        compiler_params=pltpu.CompilerParams(vmem_limit_bytes=40 * 2**20),
        name="whiten",
    )(arrived)


def shards(captured, expert_ids):
    device_count = lax.axis_size("tok") * lax.axis_size("exp")
    width = captured.shape[2]
    outbox = route(captured, expert_ids, device_count).reshape(device_count, -1, width)
    arrived = lax.all_to_all(outbox, ("tok", "exp"), split_axis=0, concat_axis=0, tiled=True)
    return whiten(arrived.reshape(-1, width))[None]


def solution(mesh):
    placed = (P(("tok", "exp"), None, None), P(("tok", "exp"), None))
    return jax.shard_map(
        shards, mesh=mesh, in_specs=placed, out_specs=P(("tok", "exp"), None, None), check_vma=False
    )
```

time: 442 us -> 109 us (0.25); the launches traced: 434 us -> 109 us
  other arithmetic: 267 us -> 0 us
  Pallas kernels: 0 us -> 65.1 us
  local copies, waits for them, and re-layouts: 62.9 us -> 1.99 us
  matrix products: 51.1 us -> 0 us
  blocking collectives: 0 us -> 41.8 us
  waiting for transfers between devices: 30.6 us -> 0 us
  starting transfers between devices: 16.6 us -> 0 us
  between operations: 6.29 us -> 0.01 us
    another operation x34 -> x0, other arithmetic: 257 us -> none  [the longest x30 172 us: whiten(): factor = jnp.linalg.cholesky(hess)]
    pallas_call x0 -> x2, Pallas kernels: none -> 65.1 us  [the longest x1 62.9 us: whiten(): pl.pallas_call(whiten_kernel, out_shape=jax.ShapeDtypeStruct((width, widt...]
    another operation x29 -> x0, matrix products: 45.5 us -> none  [the longest x14 22.9 us: whiten(): factor = jnp.linalg.cholesky(hess)]
    all_to_all x0 -> x1, blocking collectives: none -> 41.8 us  [shards(): lax.all_to_all(outbox, ('tok', 'exp'), split_axis=0, concat_axis=0, tiled...]
    another operation x34 -> x0, local copies, waits for them, and re-layouts: 31 us -> none
    all_to_all x2 -> x0, waiting for transfers between devices: 30.6 us -> none  [the longest x1 25.9 us: shards(): lax.all_to_all(outbox, ('tok', 'exp'), split_axis=0, concat_axis=0, tiled...]
    gather x1 -> x0, local copies, waits for them, and re-layouts: 16.8 us -> none  [whiten(): shift = damping * jnp.mean(jnp.diagonal(hess))]
    all_to_all x2 -> x0, starting transfers between devices: 16.6 us -> none  [the longest x1 11.5 us: shards(): lax.all_to_all(send_counts, ('tok', 'exp'), split_axis=0, concat_axis=0,...]
  transfers between devices with their start and end apart: 2 -> 0, of which waited for: 2 -> 0; matrix products, arithmetic and copies ran while one was open for 2% -> 0% of each run, Pallas kernels for 0% -> 0%
where the time goes in v1:
time: 109 us
  Pallas kernels  65.1 us (60%)
  blocking collectives  41.8 us (38%)
  local copies, waits for them, and re-layouts  1.99 us (2%)
    pallas_call x1, Pallas kernels, whiten(): pl.pallas_call(whiten_kernel, out_shape=jax.ShapeDtypeStruct((width, widt...  62.9 us
    all_to_all x1, blocking collectives, shards(): lax.all_to_all(outbox, ('tok', 'exp'), split_axis=0, concat_axis=0, tiled...  41.8 us
    pallas_call x1, Pallas kernels, route(): pl.pallas_call(lambda *refs: route_kernel(per_pair, *refs), grid=(slots /...  2.21 us

profile of v1, /device:TPU:1, one launch (start us, length us, event | category | flops | bytes accessed | tf_op | source)
XLA Modules:
  0.0 108.9 jit_solution(13280436425277282795)
XLA Ops:
  0.0 0.8 copy.3.refs_0_
  0.8 0.0 copy-start
  0.8 1.2 %copy-done = bf16[64,8,1024]{2,1,0:T(8,128)(2,1)S(1)} copy-done((bf16[64,8,1024]{2,1,0:T(8,128)(2,1)S(1)}, bf16[64,8,1024]{2,1,0:T(8,128)(2,1)}, u32[]{:S(2)}) %copy-start) | copy-done | bytes 1048600
  2.0 2.2 %route.1 = bf16[1024,1024]{1,0:T(8,128)(2,1)S(1)} custom-call(s32[64,8]{1,0:T(8,128)S(1)} %copy.3.refs_0_, bf16[512,1024]{1,0:T(8,128)(2,1)S(1)} %bitcast.6), custom_call_target="tpu_custom_call" | custom-call | tf_op jit(solution)/shard_map/route/pallas_call | solution.py:59
  4.2 41.8 %all_to_all.5 = bf16[128,8,1024]{2,1,0:T(8,128)(2,1)S(1)} all-to-all(bf16[128,8,1024]{2,1,0:T(8,128)(2,1)S(1)} %bitcast.5), channel_id=1, replica_groups=mesh['tok'=4,'exp'=32] {'tok','exp'}, dimensions={0} | all-to-all | bytes 4194304 | tf_op jit(solution)/shard_map/all_to_all | solution.py:219
  46.0 62.9 %whiten.1 = f32[1024,1024]{1,0:T(8,128)} custom-call(bf16[1024,1024]{1,0:T(8,128)(2,1)S(1)} %bitcast.4), custom_call_target="tpu_custom_call" | custom-call | tf_op jit(solution)/shard_map/whiten/pallas_call | solution.py:204
Async XLA Ops:
  0.8 1.2 %copy-start = (bf16[64,8,1024]{2,1,0:T(8,128)(2,1)S(1)}, bf16[64,8,1024]{2,1,0:T(8,128)(2,1)}, u32[]{:S(2)}) copy-start(bf16[64,8,1024]{2,1,0:T(8,128)(2,1)} %param.2) | copy-start | bytes 3145732

commit v2 on v1

--- a/solution.py
+++ b/solution.py
@@ -101,47 +101,70 @@
     return jnp.broadcast_to(x[row : row + 1, :], x.shape)
 
 
-def invert_factor(rows):
+def add_up(terms):
+    while len(terms) > 1:
+        terms = [a + b for a, b in zip(terms[::2], terms[1::2])]
+    return terms[0]
+
+
+def invert_factor(rows, beside=lambda p: None):
     lane = iota((PANEL, BLOCK), 1)
     sub = iota((PANEL, BLOCK), 0)
-    rows = list(rows)
     count = len(rows)
+    each = range(PANEL)
+    corner = [along_lanes(rows[0], j) for j in each]
     for p in range(count):
         base = p * PANEL
-        corner = [along_lanes(rows[p], base + j) for j in range(PANEL)]
-        below = {i: [along_lanes(rows[i], base + j) for j in range(PANEL)] for i in range(p + 1, count)}
+        more = p + 1 < count
+        if more:
+            beyond = [along_lanes(rows[p], base + PANEL + j) for j in each]
+            corner_next = [along_lanes(rows[p + 1], base + PANEL + j) for j in each]
+        below = {i: [along_lanes(rows[i], base + j) for j in each] for i in range(p + 1, count)}
         inside = (lane >= base) & (lane < base + PANEL)
-        forward = jnp.where(inside, jnp.where(lane == sub + base, 1.0, 0.0), rows[p])
-        full = forward
-        pivots = jnp.ones_like(forward)
-        inverses = jnp.ones_like(forward)
-        for j in range(PANEL):
-            pivot = along_sublanes(corner[j], j)
-            inverse = 1.0 / pivot
-            multiplier = jnp.where(sub == j, 0.0, corner[j] * inverse)
-            for c in range(j + 1, PANEL):
-                corner[c] = corner[c] - multiplier * along_sublanes(corner[c], j)
-            row = along_sublanes(forward, j)
-            forward = forward - jnp.where(sub > j, multiplier, 0.0) * row
-            full = full - multiplier * row
-            pivots = jnp.where(sub == j, pivot, pivots)
-            inverses = jnp.where(sub == j, inverse, inverses)
-        root = lax.rsqrt(pivots)
-        root = root * (1.5 - 0.5 * pivots * root * root)
-        rows[p] = forward * root
-        full = full * inverses
-        steps = [along_sublanes(full, j) for j in range(PANEL)]
+        full = jnp.where(inside, jnp.where(lane == sub + base, 1.0, 0.0), rows[p])
+        result = full
+        for j in range(0, PANEL, 2):
+            one, two = sub == j, sub == j + 1
+            both = one | two
+            a, b, c = (along_sublanes(corner[q], r) for q, r in ((j, j), (j + 1, j), (j + 1, j + 1)))
+            det = a * c - b * b
+            over = 1.0 / det
+            left = jnp.where(one, -1.0, jnp.where(two, 0.0, corner[j]))
+            right = jnp.where(two, -1.0, jnp.where(one, 0.0, corner[j + 1]))
+            left_over = (left * c - right * b) * over
+            right_over = (right * a - left * b) * over
+
+            def sweep(x, soon):
+                u, v = along_sublanes(x, j), along_sublanes(x, j + 1)
+                kept = jnp.where(both, 0.0, x)
+                if soon:
+                    return kept - (left * (c * u - b * v) + right * (a * v - b * u)) * over
+                return kept - (left_over * u + right_over * v)
+
+            for q in each:
+                if q not in (j, j + 1):
+                    corner[q] = sweep(corner[q], q in (j + 2, j + 3))
+            corner[j], corner[j + 1] = -left_over, -right_over
+            u, v = along_sublanes(full, j), along_sublanes(full, j + 1)
+            second = (a * v - b * u) * lax.rsqrt(a * det)
+            result = jnp.where(one, u * lax.rsqrt(a), jnp.where(two, second, result))
+            full = sweep(full, False)
+        rows[p] = result
+        if more:
+            mixed = [add_up([below[p + 1][j] * along_sublanes(corner[q], j) for j in each]) for q in each]
+            corner = [
+                corner_next[q] - add_up([mixed[j] * along_sublanes(beyond[q], j) for j in each]) for q in each
+            ]
+        steps = [along_sublanes(full, j) for j in each]
         for i in range(p + 1, count):
-            terms = [below[i][j] * steps[j] for j in range(PANEL)]
-            while len(terms) > 1:
-                terms = [a + b for a, b in zip(terms[::2], terms[1::2])]
-            rows[i] = jnp.where(inside, 0.0, rows[i]) - terms[0]
-    return rows
-
-
-def whiten_kernel(x_ref, t_ref, right_ref):
+            rows[i] = jnp.where(inside, 0.0, rows[i]) - add_up([below[i][j] * steps[j] for j in each])
+        beside(p)
+
+
+def whiten_kernel(x_ref, t_ref, left_ref, right_ref):
     width = t_ref.shape[0]
     blocks = width // BLOCK
+    panels = BLOCK // PANEL
     contract_rows = (((0,), (0,)), ((), ()))
     contract_lanes = (((1,), (1,)), ((), ()))
 
@@ -161,42 +184,91 @@
     at_origin = (iota((PANEL, BLOCK), 0) == 0) & (iota((PANEL, BLOCK), 1) == 0)
     t_ref[:PANEL, :BLOCK] = jnp.where(at_origin, square, corner)
 
+    def at(k, stop=None):
+        return slice(k * BLOCK, (k + 1 if stop is None else stop) * BLOCK)
+
     eye = iota((BLOCK, BLOCK), 0) == iota((BLOCK, BLOCK), 1)
-
-    def block(i):
-        return pl.ds(pl.multiple_of(i * BLOCK, BLOCK), BLOCK)
-
+    lower = iota((BLOCK, BLOCK), 0) >= iota((BLOCK, BLOCK), 1)
     diagonal = jnp.zeros((BLOCK, BLOCK), F32)
     for k in range(blocks):
-        diagonal = diagonal + jnp.where(eye, t_ref[block(k), block(k)], 0.0)
-    shift = damping * (jnp.sum(diagonal) / width)
-    scale = jnp.sqrt(rows_here)
-    lower = iota((BLOCK, BLOCK), 0) >= iota((BLOCK, BLOCK), 1)
-    columns = iota((BLOCK, width), 1)
-
-    def step(k, _):
-        mine = block(k)
-        spd = t_ref[mine, mine] + jnp.where(eye, shift, 0.0)
-        done = invert_factor([spd[p * PANEL : (p + 1) * PANEL] for p in range(BLOCK // PANEL)])
-        inverse = jnp.where(lower, jnp.concatenate(done, axis=0), 0.0)
+        diagonal = diagonal + jnp.where(eye, t_ref[at(k), at(k)], 0.0)
+    mean = jnp.sum(diagonal) / width
+    unit = 1.0 / mean
+    scale = jnp.sqrt(rows_here / mean)
+
+    def read(rows, columns, k):
+        return t_ref[rows, columns] * unit if k == 0 else t_ref[rows, columns]
+
+    def damped(block):
+        return block + jnp.where(eye, damping, 0.0)
+
+    spd = damped(read(at(0), at(0), 0))
+    pending = []
+
+    def beside(p):
+        for _ in range(-(-len(pending) // (panels - p))):
+            pending.pop(0)()
+
+    for k in range(blocks):
+        rows = [spd[p * PANEL : (p + 1) * PANEL] for p in range(panels)]
+        invert_factor(rows, beside)
+        inverse = jnp.where(lower, jnp.concatenate(rows, axis=0), 0.0)
+        inverse_left = left_stack(inverse)
         inverse_right = right_stack(inverse, 1)
-        t_ref[mine, mine] = jnp.where(eye, 1.0, 0.0)
-        solved = jnp.dot(left_stack(inverse), right_stack(t_ref[mine, :], 0), preferred_element_type=F32)
-        right_ref[...] = right_stack(solved, 0)
-        t_ref[mine, :] = jnp.where(columns < (k + 1) * BLOCK, solved * scale, 0.0)
-
-        def update(i, _):
-            panel = lax.dot_general(
-                left_stack(t_ref[block(i), mine]), inverse_right, contract_lanes, preferred_element_type=F32
+        if k + 1 < blocks:
+            across = jnp.dot(
+                inverse_left, right_stack(read(at(k), at(k + 1), k), 0), preferred_element_type=F32
             )
-            t_ref[block(i), mine] = jnp.zeros((BLOCK, BLOCK), F32)
-            t_ref[block(i), :] -= jnp.dot(left_stack(panel), right_ref[...], preferred_element_type=F32)
-            return 0
-
-        lax.fori_loop(k + 1, blocks, update, 0)
-        return 0
-
-    lax.fori_loop(0, blocks, step, 0)
+            down = lax.dot_general(
+                left_stack(read(at(k + 1), at(k), k)), inverse_right, contract_lanes, preferred_element_type=F32
+            )
+            spd = read(at(k + 1), at(k + 1), k)
+            if k == 0:
+                spd = damped(spd)
+            spd = spd - jnp.dot(left_stack(down), right_stack(across, 0), preferred_element_type=F32)
+
+        def solve(n, k=k, inverse=inverse, inverse_left=inverse_left):
+            for m in (n, n + 1):
+                if m == k:
+                    right_ref[:, at(m)] = right_stack(inverse, 0)
+                    t_ref[at(k), at(m)] = inverse * scale
+            if n != k and n + 1 != k:
+                parts = [(n, 2)]
+            else:
+                parts = [(n + 1 if n == k else n, 1)]
+            for m, size in parts:
+                columns = at(m, m + size)
+                solved = jnp.dot(inverse_left, right_stack(read(at(k), columns, k), 0), preferred_element_type=F32)
+                right_ref[:, columns] = right_stack(solved, 0)
+                t_ref[at(k), columns] = solved * scale if m < k else jnp.zeros_like(solved)
+
+        def descend(i, k=k, inverse_right=inverse_right):
+            left_ref[at(i), :] = left_stack(
+                lax.dot_general(
+                    left_stack(read(at(i), at(k), k)), inverse_right, contract_lanes, preferred_element_type=F32
+                )
+            )
+            t_ref[at(i), at(k)] = jnp.zeros((BLOCK, BLOCK), F32)
+
+        def update(i, n, k=k):
+            columns = at(n, n + 2)
+            before = read(at(i), columns, k)
+            if k == 0 and n <= i <= n + 1:
+                places = iota(before.shape, 1) == iota(before.shape, 0) + (i - n) * BLOCK
+                before = before + jnp.where(places, damping, 0.0)
+            t_ref[at(i), columns] = before - jnp.dot(
+                left_ref[at(i), :], right_ref[:, columns], preferred_element_type=F32
+            )
+
+        pending = [lambda n=n, solve=solve: solve(n) for n in range(0, blocks, 2)]
+        pending += [lambda i=i, descend=descend: descend(i) for i in range(k + 1, blocks)]
+        pending += [
+            lambda i=i, n=n, update=update: update(i, n)
+            for n in range(0, blocks, 2)
+            for i in range(k + 1, blocks)
+        ]
+    while pending:
+        pending.pop(0)()
 
 
 def whiten(arrived):
@@ -206,7 +278,10 @@
         out_shape=jax.ShapeDtypeStruct((width, width), F32),
         in_specs=[pl.BlockSpec(memory_space=pltpu.VMEM)],
         out_specs=pl.BlockSpec(memory_space=pltpu.VMEM),
-        scratch_shapes=[pltpu.VMEM((len(RIGHT) * BLOCK, width), BF16)],
+        scratch_shapes=[
+            pltpu.VMEM((width, len(LEFT) * BLOCK), BF16),
+            pltpu.VMEM((len(RIGHT) * BLOCK, width), BF16),
+        ],
         compiler_params=pltpu.CompilerParams(vmem_limit_bytes=40 * 2**20),
         name="whiten",
     )(arrived)

time: 109 us -> 87.9 us (0.81)
  Pallas kernels: 65.1 us -> 43.8 us
    pallas_call x1, Pallas kernels: 62.9 us -> 41.6 us  [whiten(): pl.pallas_call(whiten_kernel, out_shape=jax.ShapeDtypeStruct((width, widt...]
where the time goes in v2:
time: 87.9 us; the launch traced here: 87.7 us
  Pallas kernels  43.8 us (50%)
  blocking collectives  41.8 us (48%)
  local copies, waits for them, and re-layouts  1.99 us (2%)
    all_to_all x1, blocking collectives, shards(): lax.all_to_all(outbox, ('tok', 'exp'), split_axis=0, concat_axis=0, tiled...  41.8 us
    pallas_call x1, Pallas kernels, whiten(): pl.pallas_call(whiten_kernel, out_shape=jax.ShapeDtypeStruct((width, widt...  41.6 us
    pallas_call x1, Pallas kernels, route(): pl.pallas_call(lambda *refs: route_kernel(per_pair, *refs), grid=(slots /...  2.2 us
    unnamed x3, local copies, waits for them, and re-layouts  1.99 us

profile of v2, /device:TPU:1, one launch (start us, length us, event | category | flops | bytes accessed | tf_op | source)
XLA Modules:
  0.0 87.7 jit_solution(11535870564586490465)
XLA Ops:
  0.0 0.8 copy.3.refs_0_
  0.8 0.0 copy-start
  0.8 1.2 %copy-done = bf16[64,8,1024]{2,1,0:T(8,128)(2,1)S(1)} copy-done((bf16[64,8,1024]{2,1,0:T(8,128)(2,1)S(1)}, bf16[64,8,1024]{2,1,0:T(8,128)(2,1)}, u32[]{:S(2)}) %copy-start) | copy-done | bytes 1048600
  2.0 2.2 %route.1 = bf16[1024,1024]{1,0:T(8,128)(2,1)S(1)} custom-call(s32[64,8]{1,0:T(8,128)S(1)} %copy.3.refs_0_, bf16[512,1024]{1,0:T(8,128)(2,1)S(1)} %bitcast.6), custom_call_target="tpu_custom_call" | custom-call | tf_op jit(solution)/shard_map/route/pallas_call | solution.py:59
  4.2 41.8 %all_to_all.5 = bf16[128,8,1024]{2,1,0:T(8,128)(2,1)S(1)} all-to-all(bf16[128,8,1024]{2,1,0:T(8,128)(2,1)S(1)} %bitcast.5), channel_id=1, replica_groups=mesh['tok'=4,'exp'=32] {'tok','exp'}, dimensions={0} | all-to-all | bytes 4194304 | tf_op jit(solution)/shard_map/all_to_all | solution.py:294
  46.0 41.6 %whiten.1 = f32[1024,1024]{1,0:T(8,128)} custom-call(bf16[1024,1024]{1,0:T(8,128)(2,1)S(1)} %bitcast.4), custom_call_target="tpu_custom_call" | custom-call | tf_op jit(solution)/shard_map/whiten/pallas_call | solution.py:276
Async XLA Ops:
  0.8 1.2 %copy-start = (bf16[64,8,1024]{2,1,0:T(8,128)(2,1)S(1)}, bf16[64,8,1024]{2,1,0:T(8,128)(2,1)}, u32[]{:S(2)}) copy-start(bf16[64,8,1024]{2,1,0:T(8,128)(2,1)} %param.2) | copy-start | bytes 3145732

commit v3 on v2

v3 whole, which is shorter than its diff:
```python
import jax
import jax.numpy as jnp
from jax import lax
from jax.experimental import pallas as pl
from jax.experimental.pallas import tpu as pltpu
from jax.sharding import PartitionSpec as P

damping = 0.1
EMPTY = 32.0
BLOCK = 128
PANEL = 8
F32 = jnp.float32
BF16 = jnp.bfloat16


def iota(shape, dim):
    return lax.broadcasted_iota(jnp.int32, shape, dim)


def route_kernel(device_count, ids_ref, rows_hbm, out_ref, rows_ref, sem):
    fetch = pltpu.make_async_copy(rows_hbm, rows_ref, sem)
    fetch.start()
    top, tokens = ids_ref.shape
    entries = tokens * top
    half = entries // 2
    slots = out_ref.shape[0]
    per_pair = slots // device_count
    ids = ids_ref[...].astype(F32).astype(BF16)
    pick_col = (iota((entries, tokens), 0) // top == iota((entries, tokens), 1)).astype(F32).astype(BF16)
    by_col = lax.dot_general(pick_col, ids, (((1,), (1,)), ((), ())), preferred_element_type=F32)
    keep = iota((entries, top), 0) % top == iota((entries, top), 1)
    id_col = jnp.sum(jnp.where(keep, by_col, 0.0), axis=1, keepdims=True)
    pick_row = (iota((tokens, entries), 1) // top == iota((tokens, entries), 0)).astype(F32).astype(BF16)
    by_row = jnp.dot(ids, pick_row, preferred_element_type=F32)
    keep = iota((top, entries), 1) % top == iota((top, entries), 0)
    id_row = jnp.sum(jnp.where(keep, by_row, 0.0), axis=0, keepdims=True)
    earlier = iota((half, half), 0) < iota((half, half), 1)
    places = []
    for part in range(2):
        col = id_col[part * half : (part + 1) * half]
        row = id_row[:, part * half : (part + 1) * half]
        rank = jnp.sum(jnp.where((col == row) & earlier, 1.0, 0.0), axis=0, keepdims=True)
        places.append(row * per_pair + rank + part * (per_pair // 2))
    place = jnp.concatenate(places, axis=1).astype(jnp.int32)
    fetch.wait()
    tile = 2 * BLOCK
    for first in range(0, slots, tile):
        onehot = jnp.where(iota((tile, entries), 0) + first == place, 1.0, 0.0)
        used = jnp.sum(onehot, axis=1, keepdims=True)
        moved = jnp.dot(onehot.astype(BF16), rows_ref[...], preferred_element_type=F32)
        mark = jnp.where(iota((tile, BLOCK), 1) == 0, EMPTY * (1.0 - used), 0.0)
        out_ref[first : first + tile, :BLOCK] = (moved[:, :BLOCK] + mark).astype(BF16)
        out_ref[first : first + tile, BLOCK:] = moved[:, BLOCK:].astype(BF16)


def route(captured, expert_ids, device_count):
    token_rows, top, width = captured.shape
    slots = token_rows * top * 2
    return pl.pallas_call(
        lambda *refs: route_kernel(device_count, *refs),
        out_shape=jax.ShapeDtypeStruct((slots, width), BF16),
        in_specs=[pl.BlockSpec(memory_space=pltpu.VMEM), pl.BlockSpec(memory_space=pltpu.HBM)],
        out_specs=pl.BlockSpec(memory_space=pltpu.VMEM),
        scratch_shapes=[pltpu.VMEM((token_rows * top, width), BF16), pltpu.SemaphoreType.DMA(())],
        compiler_params=pltpu.CompilerParams(vmem_limit_bytes=32 * 2**20),
        name="route",
    )(expert_ids.T, captured.reshape(token_rows * top, width))


LEFT = (0, 0, 1, 1, 0, 2)
RIGHT = (0, 1, 0, 1, 2, 0)


def pieces(x):
    first = x.astype(BF16)
    rest = x - first.astype(F32)
    second = rest.astype(BF16)
    third = (rest - second.astype(F32)).astype(BF16)
    return first, second, third


def left_stack(x):
    part = pieces(x)
    return jnp.concatenate([part[i] for i in LEFT], axis=1)


def right_stack(x, axis):
    part = pieces(x)
    return jnp.concatenate([part[i] for i in RIGHT], axis=axis)


def along_lanes(x, lane):
    return jnp.broadcast_to(x[:, lane : lane + 1], x.shape)


def along_sublanes(x, row):
    return jnp.broadcast_to(x[row : row + 1, :], x.shape)


def add_up(terms):
    while len(terms) > 1:
        terms = [a + b for a, b in zip(terms[::2], terms[1::2])]
    return terms[0]


def invert_factor(rows, beside=lambda p: None):
    lane = iota((PANEL, BLOCK), 1)
    sub = iota((PANEL, BLOCK), 0)
    count = len(rows)
    each = range(PANEL)
    corner = [along_lanes(rows[0], j) for j in each]
    for p in range(count):
        base = p * PANEL
        more = p + 1 < count
        if more:
            beyond = [along_lanes(rows[p], base + PANEL + j) for j in each]
            corner_next = [along_lanes(rows[p + 1], base + PANEL + j) for j in each]
        below = {}

        def spread(i, base=base, below=below):
            below[i] = [along_lanes(rows[i], base + j) for j in each]

        far = list(range(p + 1, count))
        while far[:1] and far[0] <= p + 2:
            spread(far.pop(0))
        inside = (lane >= base) & (lane < base + PANEL)
        full = jnp.where(inside, jnp.where(lane == sub + base, 1.0, 0.0), rows[p])
        result = full
        for j in range(0, PANEL, 2):
            for _ in range(-(-len(far) // ((PANEL - j) // 2))):
                spread(far.pop(0))
            one, two = sub == j, sub == j + 1
            both = one | two
            a, b, c = (along_sublanes(corner[q], r) for q, r in ((j, j), (j + 1, j), (j + 1, j + 1)))
            det = a * c - b * b
            over = 1.0 / det
            left = jnp.where(one, -1.0, jnp.where(two, 0.0, corner[j]))
            right = jnp.where(two, -1.0, jnp.where(one, 0.0, corner[j + 1]))
            left_over = (left * c - right * b) * over
            right_over = (right * a - left * b) * over

            def sweep(x, soon):
                u, v = along_sublanes(x, j), along_sublanes(x, j + 1)
                kept = jnp.where(both, 0.0, x)
                if soon:
                    return kept - (left * (c * u - b * v) + right * (a * v - b * u)) * over
                return kept - (left_over * u + right_over * v)

            for q in each:
                if q not in (j, j + 1):
                    corner[q] = sweep(corner[q], q in (j + 2, j + 3))
            corner[j], corner[j + 1] = -left_over, -right_over
            u, v = along_sublanes(full, j), along_sublanes(full, j + 1)
            second = (a * v - b * u) * lax.rsqrt(a * det)
            result = jnp.where(one, u * lax.rsqrt(a), jnp.where(two, second, result))
            full = sweep(full, False)
        rows[p] = result
        if more:
            mixed = [add_up([below[p + 1][j] * along_sublanes(corner[q], j) for j in each]) for q in each]
            corner = [
                corner_next[q] - add_up([mixed[j] * along_sublanes(beyond[q], j) for j in each]) for q in each
            ]
        steps = [along_sublanes(full, j) for j in each]
        for i in range(p + 1, count):
            rows[i] = jnp.where(inside, 0.0, rows[i]) - add_up([below[i][j] * steps[j] for j in each])
        beside(p)


def whiten_kernel(x_ref, out_ref, t_ref, turned_ref, left_ref, right_ref, sems):
    total, width = x_ref.shape
    blocks = width // BLOCK
    panels = BLOCK // PANEL
    contract_lanes = (((1,), (1,)), ((), ()))

    def at(k, stop=None):
        return slice(k * BLOCK, (k + 1 if stop is None else stop) * BLOCK)

    first = iota((BLOCK, BLOCK), 1) == 0

    def squares(i, sums):
        filled, corner, trace = sums
        mine = pl.ds(pl.multiple_of(i * BLOCK, BLOCK), BLOCK)
        head = x_ref[mine, :BLOCK].astype(F32)
        real = first & (head != EMPTY)
        square = jnp.where(real, head * head, 0.0)
        filled = filled + jnp.where(real, 1.0, 0.0)
        corner = corner + square
        trace = trace + jnp.where(first, 0.0, head * head) + square
        for k in range(1, blocks):
            more = x_ref[mine, at(k)].astype(F32)
            trace = trace + more * more
        return filled, corner, trace

    sums = lax.fori_loop(0, total // BLOCK, squares, (jnp.zeros((BLOCK, BLOCK), F32),) * 3)
    rows_here, square, trace = (jnp.sum(part) for part in sums)

    eye = iota((BLOCK, BLOCK), 0) == iota((BLOCK, BLOCK), 1)
    lower = iota((BLOCK, BLOCK), 0) >= iota((BLOCK, BLOCK), 1)
    mean = trace / width
    unit = 1.0 / mean
    scale = jnp.sqrt(rows_here / mean)

    def turn(i):
        turned_ref[at(i), :] = x_ref[:, at(i)].T

    turn(0)
    spd = jnp.dot(turned_ref[at(0), :], x_ref[:, at(0)], preferred_element_type=F32)
    origin = eye & (iota((BLOCK, BLOCK), 0) == 0)
    spd = jnp.where(origin, square, spd) * unit + jnp.where(eye, damping, 0.0)

    def gram(i, n):
        mine, columns = at(i, i + 2), at(n, n + 2)
        block = jnp.dot(turned_ref[mine, :], x_ref[:, columns], preferred_element_type=F32) * unit
        if i == n:
            block = block + jnp.where(iota(block.shape, 0) == iota(block.shape, 1), damping, 0.0)
        t_ref[mine, columns] = block

    pending = [lambda i=i: turn(i) for i in range(1, blocks)]
    pending += [lambda i=i, n=n: gram(i, n) for i in range(0, blocks, 2) for n in range(0, blocks, 2)]
    sends = []

    def beside(p):
        for _ in range(-(-len(pending) // (panels - p))):
            pending.pop(0)()

    for k in range(blocks):
        rows = [spd[p * PANEL : (p + 1) * PANEL] for p in range(panels)]
        invert_factor(rows, beside)
        inverse = jnp.where(lower, jnp.concatenate(rows, axis=0), 0.0)
        inverse_left = left_stack(inverse)
        inverse_right = right_stack(inverse, 1)
        if k + 1 < blocks:
            across = jnp.dot(
                inverse_left, right_stack(t_ref[at(k), at(k + 1)], 0), preferred_element_type=F32
            )
            down = lax.dot_general(
                left_stack(t_ref[at(k + 1), at(k)]), inverse_right, contract_lanes, preferred_element_type=F32
            )
            spd = t_ref[at(k + 1), at(k + 1)] - jnp.dot(left_stack(down), right_stack(across, 0), preferred_element_type=F32)

        def solve(n, k=k, inverse=inverse, inverse_left=inverse_left):
            for m in (n, n + 1):
                if m == k:
                    right_ref[:, at(m)] = right_stack(inverse, 0)
                    t_ref[at(k), at(m)] = inverse * scale
            if n != k and n + 1 != k:
                parts = [(n, 2)]
            else:
                parts = [(n + 1 if n == k else n, 1)]
            for m, size in parts:
                columns = at(m, m + size)
                solved = jnp.dot(inverse_left, right_stack(t_ref[at(k), columns], 0), preferred_element_type=F32)
                right_ref[:, columns] = right_stack(solved, 0)
                t_ref[at(k), columns] = solved * scale if m < k else jnp.zeros_like(solved)

        def descend(i, k=k, inverse_right=inverse_right):
            left_ref[at(i), :] = left_stack(
                lax.dot_general(
                    left_stack(t_ref[at(i), at(k)]), inverse_right, contract_lanes, preferred_element_type=F32
                )
            )
            t_ref[at(i), at(k)] = jnp.zeros((BLOCK, BLOCK), F32)

        def update(i, n, k=k):
            columns = at(n, n + 2)
            t_ref[at(i), columns] -= jnp.dot(left_ref[at(i), :], right_ref[:, columns], preferred_element_type=F32)

        def send(k=k):
            sends.append(pltpu.make_async_copy(t_ref.at[at(k), :], out_ref.at[at(k), :], sems.at[k]))
            sends[-1].start()

        pending = [lambda n=n, solve=solve: solve(n) for n in range(0, blocks, 2)]
        pending += [send]
        pending += [lambda i=i, descend=descend: descend(i) for i in range(k + 1, blocks)]
        pending += [
            lambda i=i, n=n, update=update: update(i, n)
            for n in range(0, blocks, 2)
            for i in range(k + 1, blocks)
        ]
    while pending:
        pending.pop(0)()
    for copy in sends:
        copy.wait()


def whiten(arrived):
    width = arrived.shape[1]
    return pl.pallas_call(
        whiten_kernel,
        out_shape=jax.ShapeDtypeStruct((width, width), F32),
        in_specs=[pl.BlockSpec(memory_space=pltpu.VMEM)],
        out_specs=pl.BlockSpec(memory_space=pltpu.HBM),
        scratch_shapes=[
            pltpu.VMEM((width, width), F32),
            pltpu.VMEM((width, arrived.shape[0]), BF16),
            pltpu.VMEM((width, len(LEFT) * BLOCK), BF16),
            pltpu.VMEM((len(RIGHT) * BLOCK, width), BF16),
            pltpu.SemaphoreType.DMA((width // BLOCK,)),
        ],
        compiler_params=pltpu.CompilerParams(vmem_limit_bytes=40 * 2**20),
        name="whiten",
    )(arrived)


def shards(captured, expert_ids):
    device_count = lax.axis_size("tok") * lax.axis_size("exp")
    width = captured.shape[2]
    outbox = route(captured, expert_ids, device_count).reshape(device_count, -1, width)
    arrived = lax.all_to_all(outbox, ("tok", "exp"), split_axis=0, concat_axis=0, tiled=True)
    return whiten(arrived.reshape(-1, width))[None]


def solution(mesh):
    placed = (P(("tok", "exp"), None, None), P(("tok", "exp"), None))
    return jax.shard_map(
        shards, mesh=mesh, in_specs=placed, out_specs=P(("tok", "exp"), None, None), check_vma=False
    )
```

time: 87.9 us -> 84.4 us (0.960)
  Pallas kernels: 43.8 us -> 40.2 us
    pallas_call x1, Pallas kernels: 41.6 us -> 38.5 us  [whiten(): pl.pallas_call(whiten_kernel, out_shape=jax.ShapeDtypeStruct((width, widt...]
    unnamed x3 -> x4, local copies, waits for them, and re-layouts: 1.99 us -> 1.91 us
where the time goes in v3:
time: 84.4 us; the launch traced here: 84.2 us
  blocking collectives  41.8 us (50%)
  Pallas kernels  40.2 us (48%)
  local copies, waits for them, and re-layouts  1.91 us (2%)
    all_to_all x1, blocking collectives, shards(): lax.all_to_all(outbox, ('tok', 'exp'), split_axis=0, concat_axis=0, tiled...  41.8 us
    pallas_call x1, Pallas kernels, whiten(): pl.pallas_call(whiten_kernel, out_shape=jax.ShapeDtypeStruct((width, widt...  38.5 us
    unnamed x4, local copies, waits for them, and re-layouts  1.91 us
    pallas_call x1, Pallas kernels, route(): pl.pallas_call(lambda *refs: route_kernel(device_count, *refs), out_shape...  1.71 us

profile of v3, /device:TPU:1, one launch (start us, length us, event | category | flops | bytes accessed | tf_op | source)
XLA Modules:
  0.0 84.2 jit_solution(4997244131065406642)
XLA Ops:
  0.0 0.0 copy-start
  0.0 1.2 %copy-done = bf16[64,8,1024]{2,1,0:T(8,128)(2,1)S(1)} copy-done((bf16[64,8,1024]{2,1,0:T(8,128)(2,1)S(1)}, bf16[64,8,1024]{2,1,0:T(8,128)(2,1)}, u32[]{:S(2)}) %copy-start) | copy-done | bytes 1048600
  1.2 0.0 copy-start.1
  1.2 0.7 copy-done.1
  1.9 1.7 %route.1 = bf16[1024,1024]{1,0:T(8,128)(2,1)S(1)} custom-call(s32[8,64]{1,0:T(8,128)S(1)} %bitcast.8, bf16[512,1024]{1,0:T(8,128)(2,1)S(1)} %bitcast.7), custom_call_target="tpu_custom_call" | custom-call | tf_op jit(solution)/shard_map/route/pallas_call | solution.py:59
  3.6 41.8 %all_to_all.5 = bf16[128,8,1024]{2,1,0:T(8,128)(2,1)S(1)} all-to-all(bf16[128,8,1024]{2,1,0:T(8,128)(2,1)S(1)} %bitcast.6), channel_id=1, replica_groups=mesh['tok'=4,'exp'=32] {'tok','exp'}, dimensions={0} | all-to-all | bytes 4194304 | tf_op jit(solution)/shard_map/all_to_all | solution.py:309
  45.4 38.5 %whiten.1 = f32[1024,1024]{1,0:T(8,128)} custom-call(bf16[1024,1024]{1,0:T(8,128)(2,1)S(1)} %bitcast.5), custom_call_target="tpu_custom_call" | custom-call | tf_op jit(solution)/shard_map/whiten/pallas_call | solution.py:288
Async XLA Ops:
  0.0 1.2 %copy-start = (bf16[64,8,1024]{2,1,0:T(8,128)(2,1)S(1)}, bf16[64,8,1024]{2,1,0:T(8,128)(2,1)}, u32[]{:S(2)}) copy-start(bf16[64,8,1024]{2,1,0:T(8,128)(2,1)} %param.2) | copy-start | bytes 3145732
  1.2 0.7 copy-start.1

commit v4 on v3

--- a/solution.py
+++ b/solution.py
@@ -90,7 +90,7 @@
 
 
 def along_lanes(x, lane):
-    return jnp.broadcast_to(x[:, lane : lane + 1], x.shape)
+    return jnp.take_along_axis(x, jnp.full(x.shape, lane, jnp.int32), axis=1, mode="promise_in_bounds")
 
 
 def along_sublanes(x, row):
@@ -139,21 +139,18 @@
             left_over = (left * c - right * b) * over
             right_over = (right * a - left * b) * over
 
-            def sweep(x, soon):
+            def sweep(x):
                 u, v = along_sublanes(x, j), along_sublanes(x, j + 1)
-                kept = jnp.where(both, 0.0, x)
-                if soon:
-                    return kept - (left * (c * u - b * v) + right * (a * v - b * u)) * over
-                return kept - (left_over * u + right_over * v)
+                return jnp.where(both, 0.0, x) - (left_over * u + right_over * v)
 
             for q in each:
                 if q not in (j, j + 1):
-                    corner[q] = sweep(corner[q], q in (j + 2, j + 3))
+                    corner[q] = sweep(corner[q])
             corner[j], corner[j + 1] = -left_over, -right_over
             u, v = along_sublanes(full, j), along_sublanes(full, j + 1)
             second = (a * v - b * u) * lax.rsqrt(a * det)
             result = jnp.where(one, u * lax.rsqrt(a), jnp.where(two, second, result))
-            full = sweep(full, False)
+            full = sweep(full)
         rows[p] = result
         if more:
             mixed = [add_up([below[p + 1][j] * along_sublanes(corner[q], j) for j in each]) for q in each]

time: 84.4 us -> 78.5 us (0.930)
  Pallas kernels: 40.2 us -> 34.4 us
    pallas_call x1, Pallas kernels: 38.5 us -> 32.7 us  [whiten(): pl.pallas_call(whiten_kernel, out_shape=jax.ShapeDtypeStruct((width, widt...]
where the time goes in v4:
time: 78.5 us; the launch traced here: 78.3 us
  blocking collectives  41.8 us (53%)
  Pallas kernels  34.4 us (44%)
  local copies, waits for them, and re-layouts  1.91 us (2%)
    all_to_all x1, blocking collectives, shards(): lax.all_to_all(outbox, ('tok', 'exp'), split_axis=0, concat_axis=0, tiled...  41.8 us
    pallas_call x1, Pallas kernels, whiten(): pl.pallas_call(whiten_kernel, out_shape=jax.ShapeDtypeStruct((width, widt...  32.7 us
    unnamed x4, local copies, waits for them, and re-layouts  1.91 us
    pallas_call x1, Pallas kernels, route(): pl.pallas_call(lambda *refs: route_kernel(device_count, *refs), out_shape...  1.71 us

profile of v4, /device:TPU:1, one launch (start us, length us, event | category | flops | bytes accessed | tf_op | source)
XLA Modules:
  0.0 78.3 jit_solution(14075539823674198713)
XLA Ops:
  0.0 0.0 copy-start
  0.0 1.2 %copy-done = bf16[64,8,1024]{2,1,0:T(8,128)(2,1)S(1)} copy-done((bf16[64,8,1024]{2,1,0:T(8,128)(2,1)S(1)}, bf16[64,8,1024]{2,1,0:T(8,128)(2,1)}, u32[]{:S(2)}) %copy-start) | copy-done | bytes 1048600
  1.2 0.0 copy-start.1
  1.2 0.7 copy-done.1
  1.9 1.7 %route.1 = bf16[1024,1024]{1,0:T(8,128)(2,1)S(1)} custom-call(s32[8,64]{1,0:T(8,128)S(1)} %bitcast.8, bf16[512,1024]{1,0:T(8,128)(2,1)S(1)} %bitcast.7), custom_call_target="tpu_custom_call" | custom-call | tf_op jit(solution)/shard_map/route/pallas_call | solution.py:59
  3.6 41.8 %all_to_all.5 = bf16[128,8,1024]{2,1,0:T(8,128)(2,1)S(1)} all-to-all(bf16[128,8,1024]{2,1,0:T(8,128)(2,1)S(1)} %bitcast.6), channel_id=1, replica_groups=mesh['tok'=4,'exp'=32] {'tok','exp'}, dimensions={0} | all-to-all | bytes 4194304 | tf_op jit(solution)/shard_map/all_to_all | solution.py:306
  45.4 32.7 %whiten.1 = f32[1024,1024]{1,0:T(8,128)} custom-call(bf16[1024,1024]{1,0:T(8,128)(2,1)S(1)} %bitcast.5), custom_call_target="tpu_custom_call" | custom-call | tf_op jit(solution)/shard_map/whiten/pallas_call | solution.py:285
Async XLA Ops:
  0.0 1.2 %copy-start = (bf16[64,8,1024]{2,1,0:T(8,128)(2,1)S(1)}, bf16[64,8,1024]{2,1,0:T(8,128)(2,1)}, u32[]{:S(2)}) copy-start(bf16[64,8,1024]{2,1,0:T(8,128)(2,1)} %param.2) | copy-start | bytes 3145732
  1.2 0.7 copy-start.1

commit v5 on v3

--- a/solution.py
+++ b/solution.py
@@ -90,7 +90,7 @@
 
 
 def along_lanes(x, lane):
-    return jnp.broadcast_to(x[:, lane : lane + 1], x.shape)
+    return jnp.take_along_axis(x, jnp.full(x.shape, lane, jnp.int32), axis=1, mode="promise_in_bounds")
 
 
 def along_sublanes(x, row):
@@ -108,13 +108,9 @@
     sub = iota((PANEL, BLOCK), 0)
     count = len(rows)
     each = range(PANEL)
-    corner = [along_lanes(rows[0], j) for j in each]
     for p in range(count):
         base = p * PANEL
-        more = p + 1 < count
-        if more:
-            beyond = [along_lanes(rows[p], base + PANEL + j) for j in each]
-            corner_next = [along_lanes(rows[p + 1], base + PANEL + j) for j in each]
+        corner = [along_lanes(rows[p], base + j) for j in each]
         below = {}
 
         def spread(i, base=base, below=below):
@@ -126,6 +122,9 @@
         inside = (lane >= base) & (lane < base + PANEL)
         full = jnp.where(inside, jnp.where(lane == sub + base, 1.0, 0.0), rows[p])
         result = full
+        if p + 1 < count:
+            ahead = list(below[p + 1])
+            rows[p + 1] = jnp.where(inside, 0.0, rows[p + 1])
         for j in range(0, PANEL, 2):
             for _ in range(-(-len(far) // ((PANEL - j) // 2))):
                 spread(far.pop(0))
@@ -136,32 +135,32 @@
             over = 1.0 / det
             left = jnp.where(one, -1.0, jnp.where(two, 0.0, corner[j]))
             right = jnp.where(two, -1.0, jnp.where(one, 0.0, corner[j + 1]))
-            left_over = (left * c - right * b) * over
-            right_over = (right * a - left * b) * over
+            left, right = left * c - right * b, right * a - left * b
+            left_over, right_over = left * over, right * over
 
             def sweep(x, soon):
                 u, v = along_sublanes(x, j), along_sublanes(x, j + 1)
                 kept = jnp.where(both, 0.0, x)
                 if soon:
-                    return kept - (left * (c * u - b * v) + right * (a * v - b * u)) * over
+                    return kept - (left * u + right * v) * over
                 return kept - (left_over * u + right_over * v)
 
-            for q in each:
-                if q not in (j, j + 1):
-                    corner[q] = sweep(corner[q], q in (j + 2, j + 3))
-            corner[j], corner[j + 1] = -left_over, -right_over
             u, v = along_sublanes(full, j), along_sublanes(full, j + 1)
+            if p + 1 < count:
+                one_next = ahead[j] * c - ahead[j + 1] * b
+                two_next = ahead[j + 1] * a - ahead[j] * b
+                for q in range(j + 2, PANEL):
+                    term = one_next * along_sublanes(corner[q], j) + two_next * along_sublanes(corner[q], j + 1)
+                    ahead[q] = ahead[q] - term * over
+                rows[p + 1] = rows[p + 1] - (one_next * u + two_next * v) * over
+            for q in range(j + 2, PANEL):
+                corner[q] = sweep(corner[q], q <= j + 3)
             second = (a * v - b * u) * lax.rsqrt(a * det)
             result = jnp.where(one, u * lax.rsqrt(a), jnp.where(two, second, result))
-            full = sweep(full, False)
+            full = sweep(full, j + 2 == PANEL)
         rows[p] = result
-        if more:
-            mixed = [add_up([below[p + 1][j] * along_sublanes(corner[q], j) for j in each]) for q in each]
-            corner = [
-                corner_next[q] - add_up([mixed[j] * along_sublanes(beyond[q], j) for j in each]) for q in each
-            ]
         steps = [along_sublanes(full, j) for j in each]
-        for i in range(p + 1, count):
+        for i in range(p + 2, count):
             rows[i] = jnp.where(inside, 0.0, rows[i]) - add_up([below[i][j] * steps[j] for j in each])
         beside(p)
 

time: 84.4 us -> 74.2 us (0.88)
  Pallas kernels: 40.2 us -> 30.1 us
    pallas_call x1, Pallas kernels: 38.5 us -> 28.4 us  [whiten(): pl.pallas_call(whiten_kernel, out_shape=jax.ShapeDtypeStruct((width, widt...]
where the time goes in v5:
time: 74.2 us; the launch traced here: 74 us
  blocking collectives  41.8 us (56%)
  Pallas kernels  30.1 us (41%)
  local copies, waits for them, and re-layouts  1.91 us (3%)
    all_to_all x1, blocking collectives, shards(): lax.all_to_all(outbox, ('tok', 'exp'), split_axis=0, concat_axis=0, tiled...  41.8 us
    pallas_call x1, Pallas kernels, whiten(): pl.pallas_call(whiten_kernel, out_shape=jax.ShapeDtypeStruct((width, widt...  28.4 us
    unnamed x4, local copies, waits for them, and re-layouts  1.91 us
    pallas_call x1, Pallas kernels, route(): pl.pallas_call(lambda *refs: route_kernel(device_count, *refs), out_shape...  1.71 us

profile of v5, /device:TPU:1, one launch (start us, length us, event | category | flops | bytes accessed | tf_op | source)
XLA Modules:
  0.0 74.0 jit_solution(15651124465572208643)
XLA Ops:
  0.0 0.0 copy-start
  0.0 1.2 %copy-done = bf16[64,8,1024]{2,1,0:T(8,128)(2,1)S(1)} copy-done((bf16[64,8,1024]{2,1,0:T(8,128)(2,1)S(1)}, bf16[64,8,1024]{2,1,0:T(8,128)(2,1)}, u32[]{:S(2)}) %copy-start) | copy-done | bytes 1048600
  1.2 0.0 copy-start.1
  1.2 0.7 copy-done.1
  1.9 1.7 %route.1 = bf16[1024,1024]{1,0:T(8,128)(2,1)S(1)} custom-call(s32[8,64]{1,0:T(8,128)S(1)} %bitcast.8, bf16[512,1024]{1,0:T(8,128)(2,1)S(1)} %bitcast.7), custom_call_target="tpu_custom_call" | custom-call | tf_op jit(solution)/shard_map/route/pallas_call | solution.py:59
  3.6 41.8 %all_to_all.5 = bf16[128,8,1024]{2,1,0:T(8,128)(2,1)S(1)} all-to-all(bf16[128,8,1024]{2,1,0:T(8,128)(2,1)S(1)} %bitcast.6), channel_id=1, replica_groups=mesh['tok'=4,'exp'=32] {'tok','exp'}, dimensions={0} | all-to-all | bytes 4194304 | tf_op jit(solution)/shard_map/all_to_all | solution.py:308
  45.4 28.4 %whiten.1 = f32[1024,1024]{1,0:T(8,128)} custom-call(bf16[1024,1024]{1,0:T(8,128)(2,1)S(1)} %bitcast.5), custom_call_target="tpu_custom_call" | custom-call | tf_op jit(solution)/shard_map/whiten/pallas_call | solution.py:287
Async XLA Ops:
  0.0 1.2 %copy-start = (bf16[64,8,1024]{2,1,0:T(8,128)(2,1)S(1)}, bf16[64,8,1024]{2,1,0:T(8,128)(2,1)}, u32[]{:S(2)}) copy-start(bf16[64,8,1024]{2,1,0:T(8,128)(2,1)} %param.2) | copy-start | bytes 3145732
  1.2 0.7 copy-start.1

commit v6 on v5

--- a/solution.py
+++ b/solution.py
@@ -235,6 +235,8 @@
             down = lax.dot_general(
                 left_stack(t_ref[at(k + 1), at(k)]), inverse_right, contract_lanes, preferred_element_type=F32
             )
+            left_ref[at(k + 1), :] = left_stack(down)
+            t_ref[at(k + 1), at(k)] = jnp.zeros((BLOCK, BLOCK), F32)
             spd = t_ref[at(k + 1), at(k + 1)] - jnp.dot(left_stack(down), right_stack(across, 0), preferred_element_type=F32)
 
         def solve(n, k=k, inverse=inverse, inverse_left=inverse_left):
@@ -270,7 +272,7 @@
 
         pending = [lambda n=n, solve=solve: solve(n) for n in range(0, blocks, 2)]
         pending += [send]
-        pending += [lambda i=i, descend=descend: descend(i) for i in range(k + 1, blocks)]
+        pending += [lambda i=i, descend=descend: descend(i) for i in range(k + 2, blocks)]
         pending += [
             lambda i=i, n=n, update=update: update(i, n)
             for n in range(0, blocks, 2)

time: 74.2 us -> 74.1 us (level)
  no operation moved by 1% of the time
where the time goes in v6:
time: 74.1 us; the launch traced here: 73.9 us
  blocking collectives  41.8 us (56%)
  Pallas kernels  30 us (40%)
  local copies, waits for them, and re-layouts  1.91 us (3%)
    all_to_all x1, blocking collectives, shards(): lax.all_to_all(outbox, ('tok', 'exp'), split_axis=0, concat_axis=0, tiled...  41.8 us
    pallas_call x1, Pallas kernels, whiten(): pl.pallas_call(whiten_kernel, out_shape=jax.ShapeDtypeStruct((width, widt...  28.3 us
    unnamed x4, local copies, waits for them, and re-layouts  1.91 us
    pallas_call x1, Pallas kernels, route(): pl.pallas_call(lambda *refs: route_kernel(device_count, *refs), out_shape...  1.71 us

profile of v6, /device:TPU:1, one launch (start us, length us, event | category | flops | bytes accessed | tf_op | source)
XLA Modules:
  0.0 73.9 jit_solution(6839652271290782994)
XLA Ops:
  0.0 0.0 copy-start
  0.0 1.2 %copy-done = bf16[64,8,1024]{2,1,0:T(8,128)(2,1)S(1)} copy-done((bf16[64,8,1024]{2,1,0:T(8,128)(2,1)S(1)}, bf16[64,8,1024]{2,1,0:T(8,128)(2,1)}, u32[]{:S(2)}) %copy-start) | copy-done | bytes 1048600
  1.2 0.0 copy-start.1
  1.2 0.7 copy-done.1
  1.9 1.7 %route.1 = bf16[1024,1024]{1,0:T(8,128)(2,1)S(1)} custom-call(s32[8,64]{1,0:T(8,128)S(1)} %bitcast.8, bf16[512,1024]{1,0:T(8,128)(2,1)S(1)} %bitcast.7), custom_call_target="tpu_custom_call" | custom-call | tf_op jit(solution)/shard_map/route/pallas_call | solution.py:59
  3.6 41.8 %all_to_all.5 = bf16[128,8,1024]{2,1,0:T(8,128)(2,1)S(1)} all-to-all(bf16[128,8,1024]{2,1,0:T(8,128)(2,1)S(1)} %bitcast.6), channel_id=1, replica_groups=mesh['tok'=4,'exp'=32] {'tok','exp'}, dimensions={0} | all-to-all | bytes 4194304 | tf_op jit(solution)/shard_map/all_to_all | solution.py:310
  45.4 28.3 %whiten.1 = f32[1024,1024]{1,0:T(8,128)} custom-call(bf16[1024,1024]{1,0:T(8,128)(2,1)S(1)} %bitcast.5), custom_call_target="tpu_custom_call" | custom-call | tf_op jit(solution)/shard_map/whiten/pallas_call | solution.py:289
Async XLA Ops:
  0.0 1.2 %copy-start = (bf16[64,8,1024]{2,1,0:T(8,128)(2,1)S(1)}, bf16[64,8,1024]{2,1,0:T(8,128)(2,1)}, u32[]{:S(2)}) copy-start(bf16[64,8,1024]{2,1,0:T(8,128)(2,1)} %param.2) | copy-start | bytes 3145732
  1.2 0.7 copy-start.1
